TPU v7x, 32 devices: a whole 2x2x4 slice. The times are simulated.
32 devices in a mesh: section: 2 (over x), dp: 4 (over z), tensor: 4 (over y, core).
Axes of the slice: x: 2, y: 2, z: 4, core: 2. Of those that a mesh axis runs over, the one named last changes fastest.
Arguments:
- decoder_in: bfloat16 [16384, 1024], P(('section', 'dp'), 'tensor'), may hold values from -6 to 6
- encoder_out: bfloat16 [16384, 1024], P(('section', 'dp'), 'tensor'), may hold values from -6 to 6
- segments: int32 [8, 2048], P(('section', 'dp')), may hold values from 0 to 5, never falling along the last dimension, each value on 1 to 1024 neighbouring positions
- w_skip: bfloat16 [2, 1024, 1024], P(None, 'tensor'), may hold values from -0.125 to 0.125
- b_skip: float32 [1024], replicated, may hold values from -2 to 2
- ln1_gain: float32 [1024], replicated, may hold values from 0.5 to 1.5
- ln1_bias: float32 [1024], replicated, may hold values from -2 to 2
- w_qkv: bfloat16 [1024, 3, 1024], P(None, None, 'tensor'), may hold values from -0.1875 to 0.1875
- w_out: bfloat16 [1024, 1024], P('tensor'), may hold values from -0.5 to 0.5
- ln2_gain: float32 [1024], replicated, may hold values from 0.5 to 1.5
- ln2_bias: float32 [1024], replicated, may hold values from -2 to 2
- w_up: bfloat16 [1024, 4096], P(None, 'tensor'), may hold values from -0.1875 to 0.1875
- c_up: float32 [4096], P('tensor'), may hold values from -3 to 3
- w_down: bfloat16 [4096, 1024], P('tensor'), may hold values from -0.09375 to 0.09375
- cotangent: bfloat16 [16384, 1024], P(('section', 'dp')), may hold values from -6 to 6
Outputs:
- layer_out: float32 [16384, 1024], P(('section', 'dp', 'tensor'))
- d_decoder_in: float32 [16384, 1024], P(('section', 'dp'), 'tensor')
- d_encoder_out: bfloat16 [16384, 1024], P(('section', 'dp'), 'tensor')
- d_w_skip: float32 [2, 1024, 1024], P(None, 'tensor')
- d_b_skip: float32 [1024], replicated
- d_ln1_gain: float32 [1024], replicated
- d_ln1_bias: float32 [1024], replicated
- d_w_qkv: float32 [1024, 3, 1024], P(None, None, 'tensor')
- d_w_out: float32 [1024, 1024], P('tensor')
- d_ln2_gain: float32 [1024], replicated
- d_ln2_bias: float32 [1024], replicated
- d_w_up: float32 [1024, 4096], P(None, 'tensor')
- d_c_up: float32 [4096], P('tensor')
- d_w_down: float32 [4096, 1024], P('tensor')
Inputs may be any that keep to these rules, and one draw needn't show every extreme that they name: `segments`: along each packed row of 2048 frames the ids never fall; each utterance holds 1 to 1024 frames, and one of each row holds exactly 1024.
All inputs are finite; a program needn't handle non-finite values.
Results may differ from a plain program's by a relative error of at most 0.019.
Values may be sent and summed in bfloat16 or wider, within the bound.
No kernel may reach another device: no remote copies, remote signals or barrier semaphores. Data moves between devices by JAX's collectives and lax.ppermute only.
A program may use at most 192 MiB of HBM per device.

v0:
```python
import jax
import jax.numpy as jnp
from jax import lax
from jax.sharding import PartitionSpec as P

D = 1024
HEADS = 16


EPSILON = 1e-05
MASKED = -1e30
ROOT_HALF = 0.7071067811865476
INV_ROOT_TAU = 0.3989422804014327


def from_partner(value, axis, bit):
    mask = 2**bit
    pairs = [(source, source ^ mask) for source in range(lax.axis_size(axis))]
    return lax.ppermute(value, axis, pairs)


def rows_of(array, row_start, row_count):
    return lax.dynamic_slice_in_dim(array, row_start, row_count, 0)


def layer_norm(values, gain, shift):
    row_mean = jnp.mean(values, axis=-1, keepdims=True)
    centered = values - row_mean
    inv_std = lax.rsqrt(jnp.mean(centered * centered, axis=-1, keepdims=True) + EPSILON)
    normed = centered * inv_std
    return (normed * gain + shift, normed, inv_std)


def norm_back(d_output, normed, inv_std, gain):
    d_normed = d_output * gain
    d_input = inv_std * (
        d_normed
        - jnp.mean(d_normed, axis=-1, keepdims=True)
        - normed * jnp.mean(d_normed * normed, axis=-1, keepdims=True)
    )
    return (d_input, jnp.sum(d_output * normed, axis=0), jnp.sum(d_output, axis=0))


def gelu_exact(values):
    return 0.5 * values * (1.0 + lax.erf(values * ROOT_HALF))


def gelu_slope(values):
    return (
        0.5 * (1.0 + lax.erf(values * ROOT_HALF))
        + values * jnp.exp(-0.5 * values * values) * INV_ROOT_TAU
    )


def shards(
    decoder_in,
    encoder_out,
    segments,
    w_skip,
    b_skip,
    ln1_gain,
    ln1_bias,
    w_qkv,
    w_out,
    ln2_gain,
    ln2_bias,
    w_up,
    c_up,
    w_down,
    cotangent,
):
    group_rows = decoder_in.shape[0]
    tensor_ways = lax.axis_size("tensor")
    local_rows = group_rows // tensor_ways
    tensor_rank = lax.axis_index("tensor")
    heads_here = HEADS // tensor_ways
    head_dim = D // HEADS
    local_width = heads_here * head_dim
    seq_len = segments.shape[1]
    block_rows = min(512, seq_len)
    per_seq = seq_len // block_rows
    num_blocks = group_rows // block_rows
    score_scale = head_dim ** (-0.5)
    qkv_matrix = w_qkv.reshape(D, 3 * local_width)
    partner = from_partner(encoder_out, "section", 0)
    row_start = jnp.int32(0)
    merged = (
        lax.psum_scatter(
            jnp.dot(
                rows_of(decoder_in, row_start, local_rows * lax.axis_size("tensor")),
                w_skip[0],
                preferred_element_type=jnp.float32,
            )
            + jnp.dot(
                rows_of(partner, row_start, local_rows * lax.axis_size("tensor")),
                w_skip[1],
                preferred_element_type=jnp.float32,
            ),
            "tensor",
            scatter_dimension=0,
            tiled=True,
        )
        + b_skip
    )
    norm_one, normed_one, inv_std_one = layer_norm(merged, ln1_gain, ln1_bias)
    norm_one_rows = lax.all_gather(norm_one.astype(jnp.bfloat16), "tensor", axis=0, tiled=True)
    qkv = jnp.dot(norm_one_rows, qkv_matrix, preferred_element_type=jnp.float32).astype(
        jnp.bfloat16
    )
    slopes = jnp.exp2(
        -8.0
        * (tensor_rank * heads_here + jnp.arange(heads_here, dtype=jnp.int32) + 1).astype(
            jnp.float32
        )
        / HEADS
    )
    positions = jnp.arange(seq_len, dtype=jnp.int32)
    seg_flat = segments.reshape(-1)

    def scores_of(index):
        row_start = index * block_rows
        seq_start = index // per_seq * seq_len
        queries = rows_of(qkv, row_start, block_rows)[:, :local_width].reshape(
            block_rows, heads_here, head_dim
        )
        seq_block = rows_of(qkv, seq_start, seq_len)
        key_rows = seq_block[:, local_width : 2 * local_width].reshape(
            seq_len, heads_here, head_dim
        )
        val_rows = seq_block[:, 2 * local_width :].reshape(seq_len, heads_here, head_dim)
        seg_query = lax.dynamic_slice_in_dim(seg_flat, row_start, block_rows, 0)
        query_pos = row_start - seq_start + jnp.arange(block_rows, dtype=jnp.int32)
        distance = jnp.abs(query_pos[:, None] - positions[None, :]).astype(jnp.float32)
        scores = (
            jnp.einsum("qhe,khe->hqk", queries, key_rows, preferred_element_type=jnp.float32)
            * score_scale
        )
        scores = scores - slopes[:, None, None] * distance[None]
        scores = jnp.where((seg_query[:, None] == seg_flat[None, :])[None], scores, MASKED)
        return (scores, queries, key_rows, val_rows, row_start, seq_start)

    def forward_block(index):
        scores, queries, key_rows, val_rows, row_start, seq_start = scores_of(index)
        row_max = jnp.max(scores, axis=-1, keepdims=True)
        exponent = jnp.exp(scores - row_max)
        row_total = jnp.sum(exponent, axis=-1, keepdims=True)
        weights = (exponent / row_total).astype(jnp.bfloat16)
        mixed = jnp.einsum("hqk,khe->qhe", weights, val_rows, preferred_element_type=jnp.float32)
        return (mixed.reshape(block_rows, local_width), (row_max + jnp.log(row_total))[..., 0])

    mixed_blocks, log_totals = lax.map(forward_block, jnp.arange(num_blocks, dtype=jnp.int32))
    heads_out = mixed_blocks.reshape(group_rows, local_width).astype(jnp.bfloat16)
    attended = merged + lax.psum_scatter(
        jnp.dot(
            rows_of(heads_out, jnp.int32(0), local_rows * lax.axis_size("tensor")),
            w_out,
            preferred_element_type=jnp.float32,
        ),
        "tensor",
        scatter_dimension=0,
        tiled=True,
    )
    norm_two, normed_two, inv_std_two = layer_norm(attended, ln2_gain, ln2_bias)
    norm_two_rows = lax.all_gather(norm_two.astype(jnp.bfloat16), "tensor", axis=0, tiled=True)
    pre = jnp.dot(norm_two_rows, w_up, preferred_element_type=jnp.float32) + c_up
    activated = gelu_exact(pre).astype(jnp.bfloat16)
    layer_out = attended + lax.psum_scatter(
        jnp.dot(
            rows_of(activated, jnp.int32(0), local_rows * lax.axis_size("tensor")),
            w_down,
            preferred_element_type=jnp.float32,
        ).astype(jnp.bfloat16),
        "tensor",
        scatter_dimension=0,
        tiled=True,
    ).astype(jnp.float32)
    cot_local = rows_of(cotangent, tensor_rank * local_rows, local_rows).astype(jnp.float32)
    d_w_down = jnp.einsum("rf,rd->fd", activated, cotangent, preferred_element_type=jnp.float32)
    d_activated = jnp.einsum("rd,fd->rf", cotangent, w_down, preferred_element_type=jnp.float32)
    d_pre = (d_activated * gelu_slope(pre)).astype(jnp.bfloat16)
    d_w_up = jnp.einsum("rd,rf->df", norm_two_rows, d_pre, preferred_element_type=jnp.float32)
    d_c_up = jnp.sum(d_pre, axis=0, dtype=jnp.float32)
    d_norm_two = lax.psum_scatter(
        jnp.einsum(
            "rf,df->rd",
            rows_of(d_pre, jnp.int32(0), local_rows * lax.axis_size("tensor")),
            w_up,
            preferred_element_type=jnp.float32,
        ),
        "tensor",
        scatter_dimension=0,
        tiled=True,
    )
    d_attended_norm, d_gain_two, d_shift_two = norm_back(
        d_norm_two, normed_two, inv_std_two, ln2_gain
    )
    d_attended = cot_local + d_attended_norm
    d_attended_rows = lax.all_gather(d_attended.astype(jnp.bfloat16), "tensor", axis=0, tiled=True)
    d_w_out = jnp.einsum(
        "ri,rd->id", heads_out, d_attended_rows, preferred_element_type=jnp.float32
    )
    d_heads = jnp.einsum(
        "rd,id->ri", d_attended_rows, w_out, preferred_element_type=jnp.float32
    ).astype(jnp.bfloat16)

    def backward_block(carry, index):
        d_key_rows, d_val_rows = carry
        scores, queries, key_rows, val_rows, row_start, seq_start = scores_of(index)
        weights_full = jnp.exp(scores - log_totals[index][..., None])
        d_mixed = rows_of(d_heads, row_start, block_rows).reshape(block_rows, heads_here, head_dim)
        d_weights = jnp.einsum(
            "qhe,khe->hqk", d_mixed, val_rows, preferred_element_type=jnp.float32
        )
        d_scores = (
            weights_full * (d_weights - jnp.sum(weights_full * d_weights, axis=-1, keepdims=True))
        ).astype(jnp.bfloat16)
        d_queries = (
            jnp.einsum("hqk,khe->qhe", d_scores, key_rows, preferred_element_type=jnp.float32)
            * score_scale
        )
        key_part = (
            jnp.einsum("hqk,qhe->khe", d_scores, queries, preferred_element_type=jnp.float32)
            * score_scale
        )
        val_part = jnp.einsum(
            "hqk,qhe->khe",
            weights_full.astype(jnp.bfloat16),
            d_mixed,
            preferred_element_type=jnp.float32,
        )
        current_keys = rows_of(d_key_rows, seq_start, seq_len) + key_part.reshape(
            seq_len, local_width
        )
        current_vals = rows_of(d_val_rows, seq_start, seq_len) + val_part.reshape(
            seq_len, local_width
        )
        d_key_rows = current_keys
        d_val_rows = current_vals
        return ((d_key_rows, d_val_rows), d_queries.reshape(block_rows, local_width))

    empty_rows = jnp.zeros((group_rows, local_width), jnp.float32)
    (d_key_rows, d_val_rows), d_query_blocks = lax.scan(
        backward_block, (empty_rows, empty_rows), jnp.arange(num_blocks, dtype=jnp.int32)
    )
    d_qkv = jnp.concatenate(
        [d_query_blocks.reshape(group_rows, local_width), d_key_rows, d_val_rows], axis=1
    ).astype(jnp.bfloat16)
    d_w_qkv = jnp.einsum(
        "rd,rc->dc", norm_one_rows, d_qkv, preferred_element_type=jnp.float32
    ).reshape(w_qkv.shape)
    d_norm_one = lax.psum_scatter(
        jnp.einsum(
            "rc,dc->rd",
            rows_of(d_qkv, jnp.int32(0), local_rows * lax.axis_size("tensor")),
            qkv_matrix,
            preferred_element_type=jnp.float32,
        ).astype(jnp.bfloat16),
        "tensor",
        scatter_dimension=0,
        tiled=True,
    ).astype(jnp.float32)
    d_merged_norm, d_gain_one, d_shift_one = norm_back(
        d_norm_one, normed_one, inv_std_one, ln1_gain
    )
    d_merged = d_attended + d_merged_norm
    small_terms = jnp.stack(
        [jnp.sum(d_merged, axis=0), d_gain_one, d_shift_one, d_gain_two, d_shift_two]
    )
    d_merged_low = lax.all_gather(d_merged.astype(jnp.bfloat16), "tensor", axis=0, tiled=True)
    small_sum = lax.psum(small_terms, "tensor")
    d_decoder_in = jnp.einsum(
        "rd,cd->rc", d_merged_low, w_skip[0], preferred_element_type=jnp.float32
    )
    d_partner = jnp.einsum(
        "rd,cd->rc", d_merged_low, w_skip[1], preferred_element_type=jnp.float32
    ).astype(jnp.bfloat16)
    d_encoder_out = from_partner(d_partner, "section", 0)
    d_w_skip = jnp.stack(
        [
            jnp.einsum("rc,rd->cd", decoder_in, d_merged_low, preferred_element_type=jnp.float32),
            jnp.einsum("rc,rd->cd", partner, d_merged_low, preferred_element_type=jnp.float32),
        ]
    )
    d_w_skip, small_sum, d_w_qkv, d_w_out, d_w_up, d_c_up, d_w_down = lax.psum(
        (d_w_skip, small_sum, d_w_qkv, d_w_out, d_w_up, d_c_up, d_w_down), ("section", "dp")
    )
    return (
        layer_out,
        d_decoder_in,
        d_encoder_out,
        d_w_skip,
        small_sum[0],
        small_sum[1],
        small_sum[2],
        d_w_qkv,
        d_w_out,
        small_sum[3],
        small_sum[4],
        d_w_up,
        d_c_up,
        d_w_down,
    )


def solution(mesh):
    return jax.shard_map(
        shards,
        mesh=mesh,
        in_specs=(
            P(("section", "dp"), "tensor"),
            P(("section", "dp"), "tensor"),
            P(("section", "dp"), None),
            P(None, "tensor", None),
            P(),
            P(),
            P(),
            P(None, None, "tensor"),
            P("tensor", None),
            P(),
            P(),
            P(None, "tensor"),
            P("tensor"),
            P("tensor", None),
            P(("section", "dp"), None),
        ),
        out_specs=(
            P(("section", "dp", "tensor"), None),
            P(("section", "dp"), "tensor"),
            P(("section", "dp"), "tensor"),
            P(None, "tensor", None),
            P(),
            P(),
            P(),
            P(None, None, "tensor"),
            P("tensor", None),
            P(),
            P(),
            P(None, "tensor"),
            P("tensor"),
            P("tensor", None),
        ),
        check_vma=False,
    )
```

profile of v0, /device:TPU:0, one launch (start us, length us, event | category | flops | bytes accessed | tf_op | source)
XLA Modules:
  0.0 1425.6 jit_solution(11187658928478112010)
XLA Ops:
  12.9 20.8 %collective-permute-done = bf16[2048,256]{1,0:T(8,128)(2,1)S(1)} collective-permute-done((bf16[2048,256]{1,0:T(8,128)(2,1)}, bf16[2048,256]{1,0:T(8,128)(2,1)S(1)}, u32[]{:S(2)}, u32[]{:S(2)}) %collective-permute-start) | collective-permute-done | bytes 1048608 | tf_op jit(solution)/shard_map/ppermute | solution.py:19
  39.2 73.3 %reduce-scatter.6.cloned.1.call-done = f32[512,1024]{1,0:T(8,128)} async-done(((f32[2048,1024]{1,0:T(8,128)}), f32[512,1024]{1,0:T(8,128)}) %reduce-scatter.6.cloned.1.call-update) | async-done | bytes 2097168 | tf_op jit(solution)/shard_map/reduce_scatter | solution.py:88
  121.2 32.0 %all-gather.5.cloned.1.call-done = bf16[2048,1024]{1,0:T(8,128)(2,1)} async-done(((bf16[512,1024]{1,0:T(8,128)(2,1)}), bf16[2048,1024]{1,0:T(8,128)(2,1)}) %all-gather.5.cloned.1.call-update) | async-done | bytes 4194320 | tf_op jit(solution)/shard_map/all_gather | solution.py:106
  166.8 122.5 %while.32 = (s32[]{:T(128)}, bf16[4,512,256]{2,1,0:T(8,128)(2,1)}, f32[4,4,512]{2,1,0:T(4,128)S(1)}, s32[4]{0:T(128)S(1)}, s32[2048]{0:T(1024)S(1)}, /*index=5*/...) while((s32[]{:T(128)}, bf16[4,512,256]{2,1,0:T(8,128)(2,1)}, ...), condition=%wide.region_6.7_spmd.clone, body=%wide.region_3.6_spmd.clone.sunk | while | flops 1153432064 | bytes 100747792 | solution.py:151
  187.5 9.1 fusion.130
  218.0 9.1 fusion.130
  248.5 9.1 fusion.130
  279.0 9.1 fusion.130
  295.3 71.8 %reduce-scatter.8.cloned.1.call-done = f32[512,1024]{1,0:T(8,128)} async-done(((f32[2048,1024]{1,0:T(8,128)}), f32[512,1024]{1,0:T(8,128)}) %reduce-scatter.8.cloned.1.call-update) | async-done | bytes 2097168 | tf_op jit(solution)/shard_map/reduce_scatter | solution.py:153
  372.4 34.6 %all-gather.7.cloned.1.call-done = bf16[2048,1024]{1,0:T(8,128)(2,1)} async-done(((bf16[512,1024]{1,0:T(8,128)(2,1)}), bf16[2048,1024]{1,0:T(8,128)(2,1)}) %all-gather.7.cloned.1.call-update) | async-done | bytes 4194320 | tf_op jit(solution)/shard_map/all_gather | solution.py:164
  407.0 8.4 multiply_convert_fusion.1
  415.4 8.4 convert_reduce_fusion
  434.4 8.2 convolution_convert_fusion.1
  442.7 62.0 %reduce-scatter.12.cloned.1.call-done = f32[512,1024]{1,0:T(8,128)} async-done(((f32[2048,1024]{1,0:T(8,128)}), f32[512,1024]{1,0:T(8,128)}) %reduce-scatter.12.cloned.1.call-update) | async-done | bytes 2097168 | tf_op jit(solution)/shard_map/reduce_scatter | solution.py:183
  507.8 44.6 %reduce-scatter.10.cloned.1.call-done = bf16[512,1024]{1,0:T(8,128)(2,1)} async-done(((bf16[2048,1024]{1,0:T(8,128)(2,1)}), bf16[512,1024]{1,0:T(8,128)(2,1)}) %reduce-scatter.10.cloned.1.call-update) | async-done | bytes 1048592 | tf_op jit(solution)/shard_map/reduce_scatter | solution.py:167
  558.0 34.6 %all-gather.9.cloned.1.call-done = bf16[2048,1024]{1,0:T(8,128)(2,1)} async-done(((bf16[512,1024]{1,0:T(8,128)(2,1)}), bf16[2048,1024]{1,0:T(8,128)(2,1)}) %all-gather.9.cloned.1.call-update) | async-done | bytes 4194320 | tf_op jit(solution)/shard_map/all_gather | solution.py:198
  598.1 239.1 %while.33 = (s32[]{:T(128)}, f32[2048,256]{0,1:T(8,128)}, f32[2048,256]{0,1:T(8,128)}, bf16[4,512,256]{2,1,0:T(8,128)(2,1)}, s32[4]{0:T(128)S(1)}, /*index=5*/bf...) while((s32[]{:T(128)}, f32[2048,256]{0,1:T(8,128)}, ...), condition=%wide.region_16.17_spmd.clone, body=%wide.region_14.16_spmd.clone.sunk | while | flops 2737568256 | bytes 265087632 | solution.py:242
  609.1 8.1 fusion.142
  617.2 14.2 multiply_reduce_fusion.7
  631.4 11.5 multiply_convert_fusion.3
  668.8 8.1 fusion.142
  676.9 14.2 multiply_reduce_fusion.7
  691.0 11.5 multiply_convert_fusion.3
  736.6 14.2 multiply_reduce_fusion.7
  750.7 11.5 multiply_convert_fusion.3
  796.2 14.2 multiply_reduce_fusion.7
  810.4 11.5 multiply_convert_fusion.3
  848.4 44.6 %reduce-scatter.14.cloned.1.call-done = bf16[512,1024]{1,0:T(8,128)(2,1)} async-done(((bf16[2048,1024]{1,0:T(8,128)(2,1)}), bf16[512,1024]{1,0:T(8,128)(2,1)}) %reduce-scatter.14.cloned.1.call-update) | async-done | bytes 1048592 | tf_op jit(solution)/shard_map/reduce_scatter | solution.py:251
  898.6 10.2 fusion.58
  946.8 11.1 psum.57
  957.9 40.0 %all-reduce = (f32[5,1024]{1,0:T(8,128)S(1)}, f32[1024]{0:T(1024)}) all-reduce(f32[5,1024]{1,0:T(8,128)S(1)} %psum.57, f32[1024]{0:T(1024)S(1)} %copy-done.43), channel_id=1, replica_groups=mesh['section'=2,'dp'=4,'tensor'=4] {'section','dp'}, use_global_device_ids=true, to_apply=%region_27.28 | all-reduce | flops 6144 | bytes 49152 | tf_op jit(solution)/shard_map/psum | solution.py:284
  1003.6 400.5 %all-reduce.4.cloned.1.call-done = (f32[2,256,1024]{1,2,0:T(8,128)}, f32[1024,3,256]{2,0,1:T(8,128)}, f32[256,1024]{1,0:T(8,128)}, f32[1024,1024]{1,0:T(8,128)}, f32[1024,1024]{1,0:T(8,128)}) async-done(((f32[2,256,1024]{1,2,0:T(8,128)}, f32[1024,3,256]{2,0,1:T(8,128)}, f32[256,1024]{1,0:T(8,128)}, f32[1024,1024]{1,0:T(8,128)}, f32[1024,1024]{1,0:T(8,128)}), (f32[2,256,1024]{1,2,0:T(8,128)}, ...) | async-done | bytes 14680080 | tf_op jit(solution)/shard_map/psum | solution.py:284
  (344 shorter events, 316.8 us)
Async XLA Ops:
  7.2 399.8 %copy-start = (bf16[1024,1024]{1,0:T(8,128)(2,1)S(1)}, bf16[1024,1024]{1,0:T(8,128)(2,1)}, u32[]{:S(2)}) copy-start(bf16[1024,1024]{1,0:T(8,128)(2,1)} %param.30) | copy-start | bytes 6291460
  7.2 27.4 %copy-start.20 = (bf16[2,256,1024]{2,1,0:T(8,128)(2,1)S(1)}, bf16[2,256,1024]{2,1,0:T(8,128)(2,1)}, u32[]{:S(2)}) copy-start(bf16[2,256,1024]{2,1,0:T(8,128)(2,1)} %param.22) | copy-start | bytes 3145732
  7.2 105.3 %reduce-scatter.6.cloned.1.call-start = ((), (), s32[]{:S(2)}) async-start(), calls=%async_computation.5 | async-start | bytes 10485760 | tf_op jit(solution)/shard_map/reduce_scatter | solution.py:88
  7.3 26.4 %collective-permute-start = (bf16[2048,256]{1,0:T(8,128)(2,1)}, bf16[2048,256]{1,0:T(8,128)(2,1)S(1)}, u32[]{:S(2)}, u32[]{:S(2)}) collective-permute-start(bf16[2048,256]{1,0:T(8,128)(2,1)} %param.20), channel_id=1, source_target_pairs={{0,16},{16,0},{1,17},{17,1},{2,18},{18,2},{3,19},{19,3},{4,20},{20... | collective-permute-start | bytes 3145736 | tf_op jit(solution)/shard_map/ppermute | solution.py:19
  39.1 73.4 %copy-start.29 = (f32[1024]{0:T(1024)S(1)}, f32[1024]{0:T(1024)}, u32[]{:S(2)}) copy-start(f32[1024]{0:T(1024)} %param.23) | copy-start | bytes 12292
  39.2 77.9 %copy-start.35 = (f32[1024]{0:T(1024)S(1)}, f32[1024]{0:T(1024)}, u32[]{:S(2)}) copy-start(f32[1024]{0:T(1024)} %param.24) | copy-start | bytes 12292
  39.2 77.9 %copy-start.41 = (f32[1024]{0:T(1024)S(1)}, f32[1024]{0:T(1024)}, u32[]{:S(2)}) copy-start(f32[1024]{0:T(1024)} %param.25) | copy-start | bytes 12292
  39.2 114.0 %all-gather.5.cloned.1.call-start = ((), (), s32[]{:S(2)}) async-start(), calls=%async_computation.6 | async-start | bytes 5242880 | tf_op jit(solution)/shard_map/all_gather | solution.py:106
  118.5 248.6 %reduce-scatter.8.cloned.1.call-start = ((), (), s32[]{:S(2)}) async-start(), calls=%async_computation.7 | async-start | bytes 10485760 | tf_op jit(solution)/shard_map/reduce_scatter | solution.py:153
  295.2 71.9 %copy-start.30 = (f32[1024]{0:T(1024)S(1)}, f32[1024]{0:T(1024)}, u32[]{:S(2)}) copy-start(f32[1024]{0:T(1024)} %param.23) | copy-start | bytes 12292
  295.3 75.7 %copy-start.34 = (f32[1024]{0:T(1024)S(1)}, f32[1024]{0:T(1024)}, u32[]{:S(2)}) copy-start(f32[1024]{0:T(1024)} %param.28) | copy-start | bytes 12292
  295.3 75.7 %copy-start.42 = (f32[1024]{0:T(1024)S(1)}, f32[1024]{0:T(1024)}, u32[]{:S(2)}) copy-start(f32[1024]{0:T(1024)} %param.29) | copy-start | bytes 12292
  295.3 111.7 %all-gather.7.cloned.1.call-start = ((), (), s32[]{:S(2)}) async-start(), calls=%async_computation.8 | async-start | bytes 5242880 | tf_op jit(solution)/shard_map/all_gather | solution.py:164
  369.7 37.4 %copy-start.49 = (f32[1024]{0:T(1024)S(1)}, f32[1024]{0:T(1024)}, u32[]{:S(2)}) copy-start(f32[1024]{0:T(1024)} %param.31) | copy-start | bytes 12292
  372.4 132.3 %reduce-scatter.12.cloned.1.call-start = ((), (), s32[]{:S(2)}) async-start(), calls=%async_computation.10 | async-start | bytes 10485760 | tf_op jit(solution)/shard_map/reduce_scatter | solution.py:183
  432.8 119.5 %reduce-scatter.10.cloned.1.call-start = ((), (), s32[]{:S(2)}) async-start(), calls=%async_computation.9 | async-start | bytes 5242880 | tf_op jit(solution)/shard_map/reduce_scatter | solution.py:167
  442.6 62.1 %copy-start.13 = (f32[512,1024]{1,0:T(8,128)S(1)}, f32[512,1024]{1,0:T(8,128)}, u32[]{:S(2)}) copy-start(f32[512,1024]{1,0:T(8,128)} %copy-done.12) | copy-start | bytes 6291460
  442.7 149.9 %all-gather.9.cloned.1.call-start = ((), (), s32[]{:S(2)}) async-start(), calls=%async_computation.11 | async-start | bytes 5242880 | tf_op jit(solution)/shard_map/all_gather | solution.py:198
  552.4 40.2 %copy-start.27 = (bf16[256,1024]{1,0:T(8,128)(2,1)S(1)}, bf16[256,1024]{1,0:T(8,128)(2,1)}, u32[]{:S(2)}) copy-start(bf16[256,1024]{1,0:T(8,128)(2,1)} %param.27) | copy-start | bytes 1572868
  557.9 335.0 %reduce-scatter.14.cloned.1.call-start = ((), (), s32[]{:S(2)}) async-start(), calls=%async_computation.12 | async-start | bytes 5242880 | tf_op jit(solution)/shard_map/reduce_scatter | solution.py:251
  631.4 15.4 %copy-start.2 = (f32[4,512,2048]{2,1,0:T(8,128)S(1)}, f32[4,512,2048]{2,1,0:T(8,128)}, u32[]{:S(2)}) copy-start(f32[4,512,2048]{2,1,0:T(8,128)} %get-tuple-element.628) | copy-start | bytes 50331652 | tf_op jit(solution)/shard_map/while
  691.0 15.4 %copy-start.2 = (f32[4,512,2048]{2,1,0:T(8,128)S(1)}, f32[4,512,2048]{2,1,0:T(8,128)}, u32[]{:S(2)}) copy-start(f32[4,512,2048]{2,1,0:T(8,128)} %get-tuple-element.628) | copy-start | bytes 50331652 | tf_op jit(solution)/shard_map/while
  750.7 15.4 %copy-start.2 = (f32[4,512,2048]{2,1,0:T(8,128)S(1)}, f32[4,512,2048]{2,1,0:T(8,128)}, u32[]{:S(2)}) copy-start(f32[4,512,2048]{2,1,0:T(8,128)} %get-tuple-element.628) | copy-start | bytes 50331652 | tf_op jit(solution)/shard_map/while
  848.2 44.7 %copy-start.11 = (f32[512,1024]{1,0:T(8,128)S(1)}, f32[512,1024]{1,0:T(8,128)}, u32[]{:S(2)}) copy-start(f32[512,1024]{1,0:T(8,128)} %reduce-scatter.6.cloned.1.call-done) | copy-start | bytes 6291460
  848.3 44.7 %copy-start.31 = (f32[1024]{0:T(1024)S(1)}, f32[1024]{0:T(1024)}, u32[]{:S(2)}) copy-start(f32[1024]{0:T(1024)} %param.23) | copy-start | bytes 12292
  848.3 44.7 %copy-start.33 = (f32[512]{0:T(512)S(1)}, f32[512]{0:T(512)}, u32[]{:S(2)}) copy-start(f32[512]{0:T(512)} %copy-done.32) | copy-start | bytes 6148
  848.3 44.7 %copy-start.36 = (f32[1024]{0:T(1024)S(1)}, f32[1024]{0:T(1024)}, u32[]{:S(2)}) copy-start(f32[1024]{0:T(1024)} %param.24) | copy-start | bytes 12292
  848.3 44.7 %copy-start.38 = (f32[512]{0:T(512)S(1)}, f32[512]{0:T(512)}, u32[]{:S(2)}) copy-start(f32[512]{0:T(512)} %copy-done.37) | copy-start | bytes 6148
  848.3 84.8 %all-gather.11.cloned.1.call-start = ((), (), s32[]{:S(2)}) async-start(), calls=%async_computation.13 | async-start | bytes 5242880 | tf_op jit(solution)/shard_map/all_gather | solution.py:269
  898.5 505.6 %all-reduce.4.cloned.1.call-start = ((), (), s32[]{:S(2)}) async-start(), calls=%async_computation.14 | async-start | bytes 29360128 | tf_op jit(solution)/shard_map/psum | solution.py:284
  940.8 17.1 %copy-start.43 = (f32[1024]{0:T(1024)S(1)}, f32[1024]{0:T(1024)}, u32[]{:S(2)}) copy-start(f32[1024]{0:T(1024)} %get-tuple-element.490) | copy-start | bytes 12292
  945.3 58.4 %collective-permute-start.1 = (bf16[2048,256]{1,0:T(8,128)(2,1)}, bf16[2048,256]{1,0:T(8,128)(2,1)S(1)}, u32[]{:S(2)}, u32[]{:S(2)}) collective-permute-start(bf16[2048,256]{1,0:T(8,128)(2,1)} %convolution_convert_fusion.3), channel_id=1, source_target_pairs={{0,16},{16,0},{1,17},{17,1},{2,18},{18,2},{3,19},{19,3},{4,20},{20... | collective-permute-start | bytes 3145736 | tf_op jit(solution)/shard_map/ppermute | solution.py:19
  (53 other events, 235.5 us)
Sparse Core Ops, SparseCore 0:
  39.3 73.1 reduce-scatter.5
  118.7 34.4 all-gather.4
  295.4 71.6 reduce-scatter.7
  372.5 34.4 all-gather.6
  433.0 71.7 reduce-scatter.11
  507.8 44.5 reduce-scatter.9
  558.1 34.4 all-gather.8
  848.4 44.4 reduce-scatter.13
  898.6 34.4 all-gather.10
  940.1 463.9 all-reduce.3
where the time goes:
time: 1440 us; the launch traced here: 1430 us
  waiting for transfers between devices  823 us (57%)
  matrix products  275 us (19%)
  local copies, waits for them, and re-layouts  112 us (8%)
  other arithmetic  110 us (8%)
  blocking collectives  51.1 us (4%)
  loops' own time  34.1 us (2%)
  between operations  14.7 us (1%)
    psum x1, waiting for transfers between devices, shards(): lax.psum((d_w_skip, small_sum, d_w_qkv, d_w_out, d_w_up, d_c_up, d_w_down...  400 us
    dot_general x8, matrix products, scores_of(): jnp.einsum('qhe,khe->hqk', queries, key_rows, preferred_element_type=jnp....  77.5 us
    reduce_scatter x1, waiting for transfers between devices, shards(): lax.psum_scatter(jnp.dot(rows_of(decoder_in, row_start, local_rows * lax....  73.3 us
    reduce_scatter x1, waiting for transfers between devices, shards(): lax.psum_scatter(jnp.dot(rows_of(heads_out, jnp.int32(0), local_rows * la...  71.8 us
    reduce_scatter x1, waiting for transfers between devices, shards(): lax.psum_scatter(jnp.einsum('rf,df->rd', rows_of(d_pre, jnp.int32(0), loc...  62 us
    convert_element_type x4, other arithmetic, backward_block(): d_scores = (weights_full * (d_weights - jnp.sum(weights_full * d_weights,...  45.9 us
    reduce_scatter x1, waiting for transfers between devices, shards(): lax.psum_scatter(jnp.einsum('rc,dc->rd', rows_of(d_qkv, jnp.int32(0), loc...  44.6 us
    reduce_scatter x1, waiting for transfers between devices, shards(): lax.psum_scatter(jnp.dot(rows_of(activated, jnp.int32(0), local_rows * la...  44.6 us
  transfers between devices with their start and end apart: 12, of which 11 were waited for; matrix products, arithmetic and copies ran while one was open for 4% of the time, Pallas kernels for 0%

commit v1 on v0

v1 whole, which is shorter than its diff:
```python
import functools
import jax
import jax.numpy as jnp
from jax import lax
from jax.experimental import pallas as pl
from jax.experimental.pallas import tpu as pltpu
from jax.sharding import PartitionSpec as P

D = 1024
HEADS = 16
UTTS = 6
HEAD_DIM = D // HEADS
SCALE = HEAD_DIM**-0.5

EPSILON = 1e-05
FAR = 1e30
ROOT_HALF = 0.7071067811865476
INV_ROOT_TAU = 0.3989422804014327
BF16 = jnp.bfloat16
F32 = jnp.float32
NT = (((1,), (1,)), ((), ()))
NN = (((1,), (0,)), ((), ()))
TN = (((0,), (0,)), ((), ()))
CHUNKS = 2


def mm(left, right, dims):
    return lax.dot_general(left, right, dims, preferred_element_type=F32)


def starts_of(seg):
    return [jnp.sum((seg < u).astype(jnp.int32)) for u in range(1, UTTS)]


def tile_range(starts, first, count, tile, total):
    low = jnp.int32(0)
    high = jnp.int32(total)
    for s in starts:
        low = jnp.maximum(low, jnp.where(s <= first, s, 0))
        high = jnp.minimum(high, jnp.where(s >= first + count, s, total))
    return low // tile, (high + tile - 1) // tile


def eye(n):
    r = lax.broadcasted_iota(jnp.int32, (n, n), 0)
    c = lax.broadcasted_iota(jnp.int32, (n, n), 1)
    return jnp.where(r == c, 1.0, 0.0).astype(BF16)


def far_tile(starts, seg_row, q_first, k_first, bk, bq):
    kpos = k_first + lax.broadcasted_iota(jnp.int32, (bk, bq), 0)
    qpos = q_first + lax.broadcasted_iota(jnp.int32, (bk, bq), 1)
    lo = jnp.zeros_like(seg_row)
    hi = jnp.full_like(seg_row, starts[0])
    for u in range(1, UTTS):
        lo = jnp.where(seg_row == u, starts[u - 1], lo)
        hi = jnp.where(seg_row == u, starts[u] if u < UTTS - 1 else 1 << 30, hi)
    ok = (kpos >= lo) & (kpos < hi)
    return jnp.where(ok, jnp.abs(kpos - qpos).astype(F32), FAR)


def head_masked(pair, which):
    lane = lax.broadcasted_iota(jnp.int32, pair.shape, 1)
    keep = (lane < HEAD_DIM) if which == 0 else (lane >= HEAD_DIM)
    return jnp.where(keep, pair, 0.0).astype(BF16)


def load_pieces(core, pieces, whole_ref, sems):
    copies = []
    rows = pieces[0].shape[1]
    for n, piece in enumerate(pieces):
        chunk, side = n // 2, n % 2
        for y in range(2):
            first = y * (4 * rows) + (core ^ side) * (2 * rows) + chunk * rows
            copy = pltpu.make_async_copy(
                piece.at[y], whole_ref.at[pl.ds(pl.multiple_of(first, rows), rows)], sems.at[n, y]
            )
            copy.start()
            copies.append(copy)
    for copy in copies:
        copy.wait()


def fwd_kernel(
    heads, bk, chunk, core_ref, slope_ref, seg_ref, q00, q01, q10, q11,
    out_ref, lse_ref, qkv_ref, vt_ref, acc_ref, s_ref, top_ref, sems,
):
    total = seg_ref.shape[1]
    width = heads * HEAD_DIM
    bq = out_ref.shape[1] // 2
    core = core_ref[0]
    load_pieces(core, (q00, q01, q10, q11), qkv_ref, sems)
    starts = starts_of(seg_ref[...])
    ident = eye(width)

    def prep(j, c):
        at = pl.ds(pl.multiple_of(j * bk, bk), bk)
        vt = mm(ident, qkv_ref[at, 2 * width : 3 * width], NT).astype(BF16)
        for h in range(heads):
            vt_ref[h * 80 : h * 80 + 64, at] = vt[h * 64 : (h + 1) * 64]
            vt_ref[h * 80 + 64 : (h + 1) * 80, at] = jnp.ones((16, bk), BF16)
        return c

    lax.fori_loop(0, total // bk, prep, 0)

    def q_step(i, c):
        side, y = i // 2, i % 2
        qi = pl.multiple_of(y * (4 * bq) + (core ^ side) * (2 * bq) + chunk * bq, bq)
        lo, hi = tile_range(starts, qi, bq, bk, total)
        seg_row = seg_ref[:, pl.ds(qi, bq)]
        acc_ref[...] = jnp.zeros_like(acc_ref)
        top_ref[...] = jnp.full_like(top_ref, -3e38)
        qs = []
        for h in range(heads):
            p = h // 2
            qp = qkv_ref[pl.ds(qi, bq), p * 128 : (p + 1) * 128].astype(F32) * SCALE
            qs.append(head_masked(qp, h % 2))

        def score_step(j, c):
            kj = pl.multiple_of(j * bk, bk)
            far = far_tile(starts, seg_row, qi, kj, bk, bq)
            for h in range(heads):
                p = h // 2
                kp = qkv_ref[pl.ds(kj, bk), width + p * 128 : width + (p + 1) * 128]
                s = mm(kp, qs[h], NT) - far * slope_ref[h]
                s_ref[h, pl.ds(kj, bk)] = s
                top_ref[h] = jnp.maximum(top_ref[h], jnp.max(s.reshape(bk // 8, 8, bq), axis=0))
            return c

        lax.fori_loop(lo, hi, score_step, 0)
        tops = [jnp.max(top_ref[h], axis=0, keepdims=True) for h in range(heads)]

        def mix_step(j, c):
            kj = pl.multiple_of(j * bk, bk)
            for h in range(heads):
                e = jnp.exp(s_ref[h, pl.ds(kj, bk)] - tops[h]).astype(BF16)
                hs = slice(h * 80, (h + 1) * 80)
                acc_ref[hs] = acc_ref[hs] + mm(vt_ref[hs, pl.ds(kj, bk)], e, NN)
            return c

        lax.fori_loop(lo, hi, mix_step, 0)
        outs = []
        for h in range(heads):
            whole = acc_ref[h * 80 + 64 : h * 80 + 65]
            outs.append((acc_ref[h * 80 : h * 80 + 64] * (1.0 / whole)).astype(BF16))
            lse_ref[i, h : h + 1] = tops[h] + jnp.log(whole)
        ot = jnp.concatenate(outs, axis=0)
        out_ref[side, pl.ds(pl.multiple_of(y * bq, bq), bq)] = mm(eye(bq), ot, NT).astype(BF16)
        return c

    lax.fori_loop(0, 4, q_step, 0)


def attend(chunk, core, slopes, seg, pieces):
    total = seg.shape[1]
    rows = pieces[0].shape[1]
    heads = pieces[0].shape[2] // (3 * HEAD_DIM)
    width = heads * HEAD_DIM
    bk = 256
    smem = pl.BlockSpec(memory_space=pltpu.SMEM)
    vmem = pl.BlockSpec(memory_space=pltpu.VMEM)
    hbm = pl.BlockSpec(memory_space=pl.ANY)
    return pl.pallas_call(
        functools.partial(fwd_kernel, heads, bk, chunk),
        out_shape=(
            jax.ShapeDtypeStruct((2, 2 * rows, width), BF16),
            jax.ShapeDtypeStruct((4, heads, rows), F32),
        ),
        in_specs=[smem, smem, vmem] + [hbm] * 4,
        out_specs=(vmem, vmem),
        scratch_shapes=[
            pltpu.VMEM((total, 3 * width), BF16),
            pltpu.VMEM((heads * 80, total), BF16),
            pltpu.VMEM((heads * 80, rows), F32),
            pltpu.VMEM((heads, total, rows), F32),
            pltpu.VMEM((heads, 8, rows), F32),
            pltpu.SemaphoreType.DMA((4, 2)),
        ],
        compiler_params=pltpu.CompilerParams(vmem_limit_bytes=40 << 20),
        name="attend",
    )(core, slopes, seg, *pieces)


def bwd_kernel(heads, bk, chunk, *refs):
    core_ref, slope_ref, seg_ref, q00, q01, q10, q11, do0, do1, o_ref, lse_ref = refs[:11]
    if chunk == 0:
        dq_ref, dkv_ref = refs[11:13]
        rest = refs[13:]
    else:
        dq_in, dkv_in, dqkv_ref = refs[11:14]
        rest = refs[14:]
    qkv_ref, kt_ref, dqt_ref, dk_ref, dv_ref, delta_ref, sems = rest
    total = seg_ref.shape[1]
    width = heads * HEAD_DIM
    bq = o_ref.shape[1] // 2
    core = core_ref[0]
    load_pieces(core, (q00, q01, q10, q11), qkv_ref, sems)
    starts = starts_of(seg_ref[...])
    ident = eye(width)
    hr = lax.broadcasted_iota(jnp.int32, (8, width), 0)
    hc = lax.broadcasted_iota(jnp.int32, (8, width), 1)
    pick = jnp.where(hr == hc // HEAD_DIM, 1.0, 0.0)

    def prep(j, c):
        at = pl.ds(pl.multiple_of(j * bk, bk), bk)
        kj = qkv_ref[at, width : 2 * width]
        kt_ref[:, at] = (mm(ident, kj, NT) * SCALE).astype(BF16)
        if chunk == 0:
            dk_ref[at] = jnp.zeros((bk, width), F32)
            dv_ref[at] = jnp.zeros((bk, width), F32)
        else:
            dk_ref[at] = dkv_in[at, :width]
            dv_ref[at] = dkv_in[at, width:]
        return c

    lax.fori_loop(0, total // bk, prep, 0)
    for side, do_ref in enumerate((do0, do1)):
        for y in range(2):
            at = slice(y * bq, (y + 1) * bq)
            prod = do_ref[at].astype(F32) * o_ref[side, at].astype(F32)
            delta_ref[side * 2 + y] = lax.dot_general(
                pick, prod, NT, precision=lax.Precision.HIGHEST, preferred_element_type=F32
            )

    for side, do_ref in enumerate((do0, do1)):

        def q_step(y, c, side=side, do_ref=do_ref):
            i = side * 2 + y
            qi = pl.multiple_of(y * (4 * bq) + (core ^ side) * (2 * bq) + chunk * bq, bq)
            here = pl.ds(pl.multiple_of(y * bq, bq), bq)
            lo, hi = tile_range(starts, qi, bq, bk, total)
            seg_row = seg_ref[:, pl.ds(qi, bq)]
            dqt_ref[...] = jnp.zeros_like(dqt_ref)
            qs, dos = [], []
            for h in range(heads):
                p = h // 2
                qp = qkv_ref[pl.ds(qi, bq), p * 128 : (p + 1) * 128].astype(F32) * SCALE
                qs.append(head_masked(qp, h % 2))
                dp = do_ref[here, p * 128 : (p + 1) * 128].astype(F32)
                dos.append(head_masked(dp, h % 2))
            lses = [lse_ref[i, h : h + 1] for h in range(heads)]
            deltas = [delta_ref[i, h : h + 1] for h in range(heads)]

            def k_step(j, c):
                kj = pl.multiple_of(j * bk, bk)
                at = pl.ds(kj, bk)
                far = far_tile(starts, seg_row, qi, kj, bk, bq)
                for p in range(heads // 2):
                    cols = slice(p * 128, (p + 1) * 128)
                    kp = qkv_ref[at, width + p * 128 : width + (p + 1) * 128]
                    vp = qkv_ref[at, 2 * width + p * 128 : 2 * width + (p + 1) * 128]
                    dv = dv_ref[at, cols]
                    dk = dk_ref[at, cols]
                    for h in (2 * p, 2 * p + 1):
                        s = mm(kp, qs[h], NT) - far * slope_ref[h]
                        w = jnp.exp(s - lses[h])
                        dw = mm(vp, dos[h], NT)
                        ds = (w * (dw - deltas[h])).astype(BF16)
                        dv = dv + mm(w.astype(BF16), dos[h], NN)
                        dk = dk + mm(ds, qs[h], NN)
                        hs = slice(h * HEAD_DIM, (h + 1) * HEAD_DIM)
                        dqt_ref[hs] = dqt_ref[hs] + mm(kt_ref[hs, at], ds, NN)
                    dv_ref[at, cols] = dv
                    dk_ref[at, cols] = dk
                return c

            lax.fori_loop(lo, hi, k_step, 0)
            dq = mm(eye(bq), dqt_ref[...].astype(BF16), NT).astype(BF16)
            if chunk == 0:
                dq_ref[side, here] = dq
            else:
                dqkv_ref[2 + side, here, :width] = dq
            return c

        lax.fori_loop(0, 2, q_step, 0)

    if chunk == 0:

        def finish(j, c):
            at = pl.ds(pl.multiple_of(j * bk, bk), bk)
            dkv_ref[at, :width] = dk_ref[at]
            dkv_ref[at, width:] = dv_ref[at]
            return c

        lax.fori_loop(0, total // bk, finish, 0)
    else:
        for side in range(2):
            dqkv_ref[side, :, :width] = dq_in[side]
        for n in range(4):
            part, side = n // 2, n % 2
            for y in range(2):
                first = y * (4 * bq) + (core ^ side) * (2 * bq) + part * bq
                at = pl.ds(pl.multiple_of(first, bq), bq)
                here = slice(y * bq, (y + 1) * bq)
                dqkv_ref[n, here, width : 2 * width] = dk_ref[at].astype(BF16)
                dqkv_ref[n, here, 2 * width :] = dv_ref[at].astype(BF16)


def attend_back(chunk, core, slopes, seg, pieces, d_heads, heads_out, lse, before=()):
    total = seg.shape[1]
    rows = pieces[0].shape[1]
    heads = pieces[0].shape[2] // (3 * HEAD_DIM)
    width = heads * HEAD_DIM
    bk = 256
    smem = pl.BlockSpec(memory_space=pltpu.SMEM)
    vmem = pl.BlockSpec(memory_space=pltpu.VMEM)
    hbm = pl.BlockSpec(memory_space=pl.ANY)
    if chunk == 0:
        out_shape = (
            jax.ShapeDtypeStruct((2, 2 * rows, width), BF16),
            jax.ShapeDtypeStruct((total, 2 * width), F32),
        )
        out_specs = (vmem, vmem)
    else:
        out_shape = jax.ShapeDtypeStruct((4, 2 * rows, 3 * width), BF16)
        out_specs = vmem
    return pl.pallas_call(
        functools.partial(bwd_kernel, heads, bk, chunk),
        out_shape=out_shape,
        in_specs=[smem, smem, vmem] + [hbm] * 4 + [vmem] * (4 + len(before)),
        out_specs=out_specs,
        scratch_shapes=[
            pltpu.VMEM((total, 3 * width), BF16),
            pltpu.VMEM((width, total), BF16),
            pltpu.VMEM((width, rows), F32),
            pltpu.VMEM((total, width), F32),
            pltpu.VMEM((total, width), F32),
            pltpu.VMEM((4, 8, rows), F32),
            pltpu.SemaphoreType.DMA((4, 2)),
        ],
        compiler_params=pltpu.CompilerParams(vmem_limit_bytes=48 << 20),
        name="attend_back",
    )(core, slopes, seg, *pieces, *d_heads, heads_out, lse, *before)


def swap(value, axis, bit):
    pairs = [(source, source ^ (1 << bit)) for source in range(lax.axis_size(axis))]
    return lax.ppermute(value, axis, pairs)


core_swap = functools.partial(swap, axis="tensor", bit=0)
chip_swap = functools.partial(swap, axis="tensor", bit=1)
partner_swap = functools.partial(swap, axis="section", bit=0)


def add_low(*terms):
    return sum(term.astype(F32) for term in terms).astype(BF16)


def group_steps():
    steps = [("section", 0)]
    for bit in range((lax.axis_size("dp") - 1).bit_length()):
        steps.append(("dp", bit))
    return steps


def group_sum(value, steps):
    sides = []
    for axis, bit in steps:
        mine = (lax.axis_index(axis) >> bit) & 1
        halves = value.reshape(2, value.shape[0] // 2, value.shape[1])
        sent = lax.dynamic_index_in_dim(halves, 1 - mine, 0, keepdims=False)
        kept = lax.dynamic_index_in_dim(halves, mine, 0, keepdims=False)
        value = add_low(kept, swap(sent, axis, bit))
        sides.append((axis, bit, mine))
    for axis, bit, mine in reversed(sides):
        other = swap(value, axis, bit)
        first = mine == 0
        value = jnp.concatenate(
            [jnp.where(first, value, other), jnp.where(first, other, value)], axis=0
        )
    return value


def layer_norm(values, gain, shift):
    row_mean = jnp.mean(values, axis=-1, keepdims=True)
    centered = values - row_mean
    inv_std = lax.rsqrt(jnp.mean(centered * centered, axis=-1, keepdims=True) + EPSILON)
    normed = centered * inv_std
    return (normed * gain + shift, normed, inv_std)


def norm_back(d_output, normed, inv_std, gain):
    d_normed = d_output * gain
    d_input = inv_std * (
        d_normed
        - jnp.mean(d_normed, axis=-1, keepdims=True)
        - normed * jnp.mean(d_normed * normed, axis=-1, keepdims=True)
    )
    return (d_input, jnp.sum(d_output * normed, axis=0), jnp.sum(d_output, axis=0))


def gelu_exact(values):
    return 0.5 * values * (1.0 + lax.erf(values * ROOT_HALF))


def gelu_slope(values):
    return (
        0.5 * (1.0 + lax.erf(values * ROOT_HALF))
        + values * jnp.exp(-0.5 * values * values) * INV_ROOT_TAU
    )


def shards(
    decoder_in,
    encoder_out,
    segments,
    w_skip,
    b_skip,
    ln1_gain,
    ln1_bias,
    w_qkv,
    w_out,
    ln2_gain,
    ln2_bias,
    w_up,
    c_up,
    w_down,
    cotangent,
):
    group_rows = decoder_in.shape[0]
    tensor_rank = lax.axis_index("tensor")
    core = tensor_rank & 1
    chip = tensor_rank >> 1
    heads_here = HEADS // lax.axis_size("tensor")
    local_width = heads_here * HEAD_DIM
    block = group_rows // (4 * CHUNKS)
    qkv_matrix = w_qkv.reshape(D, 3 * local_width)
    core_scalar = core.reshape(1).astype(jnp.int32)
    slopes = jnp.exp2(
        -8.0
        * (tensor_rank * heads_here + jnp.arange(heads_here, dtype=jnp.int32) + 1).astype(F32)
        / HEADS
    )
    spots = [(chunk, side) for chunk in range(CHUNKS) for side in range(2)]

    def piece_of(array, chunk, side):
        width = array.shape[-1]
        parts = array.reshape(2, 2, CHUNKS, block, width)[:, :, chunk]
        return lax.dynamic_index_in_dim(parts, core ^ side, 1, keepdims=False).reshape(
            2 * block, width
        )

    def whole_of(pieces):
        width = pieces[0].shape[-1]
        sides = []
        for side in range(2):
            sides.append(
                jnp.stack(
                    [pieces[2 * n + side].reshape(2, block, width) for n in range(CHUNKS)], axis=1
                )
            )
        zero = core == 0
        return jnp.stack(
            [jnp.where(zero, sides[0], sides[1]), jnp.where(zero, sides[1], sides[0])], axis=1
        ).reshape(group_rows, width)

    encoder_parts = encoder_out.reshape(2, 2, CHUNKS, block, encoder_out.shape[1])
    partner = [
        partner_swap(encoder_parts[:, :, chunk].reshape(4 * block, -1)) for chunk in range(CHUNKS)
    ]

    def partner_piece(chunk, side):
        parts = partner[chunk].reshape(2, 2, block, -1)
        return lax.dynamic_index_in_dim(parts, core ^ side, 1, keepdims=False).reshape(
            2 * block, -1
        )

    merged, normed_one, inv_std_one, norm_one, qkv = [], [], [], {}, {}
    for chunk in range(CHUNKS):
        halves = [
            (
                jnp.dot(piece_of(decoder_in, chunk, side), w_skip[0], preferred_element_type=F32)
                + jnp.dot(partner_piece(chunk, side), w_skip[1], preferred_element_type=F32)
            ).astype(BF16)
            for side in range(2)
        ]
        chip_sum = add_low(halves[0], core_swap(halves[1]))
        value = chip_sum.astype(F32) + chip_swap(chip_sum).astype(F32) + b_skip
        normal, normed, inv_std = layer_norm(value, ln1_gain, ln1_bias)
        merged.append(value)
        normed_one.append(normed)
        inv_std_one.append(inv_std)
        normal = normal.astype(BF16)
        norm_one[chunk, 0] = normal
        norm_one[chunk, 1] = core_swap(normal)
        for side in range(2):
            qkv[chunk, side] = jnp.dot(
                norm_one[chunk, side], qkv_matrix, preferred_element_type=F32
            ).astype(BF16)
    qkv_pieces = [qkv[spot].reshape(2, block, 3 * local_width) for spot in spots]

    heads_out, lse, attended, d_attended, d_attended_rows = [], [], [], [], {}
    gain_two_sum = shift_two_sum = c_up_sum = 0.0
    norm_two, activated, d_pre, cot = {}, {}, {}, {}
    normed_two, inv_std_two = [], []
    for chunk in range(CHUNKS):
        mixed, log_total = attend(chunk, core_scalar, slopes, segments, qkv_pieces)
        heads_out.append(mixed)
        lse.append(log_total)
        halves = [
            jnp.dot(mixed[side], w_out, preferred_element_type=F32).astype(BF16)
            for side in range(2)
        ]
        chip_sum = add_low(halves[0], core_swap(halves[1]))
        value = merged[chunk] + (chip_sum.astype(F32) + chip_swap(chip_sum).astype(F32))
        attended.append(value)
        normal, normed, inv_std = layer_norm(value, ln2_gain, ln2_bias)
        normed_two.append(normed)
        inv_std_two.append(inv_std)
        normal = normal.astype(BF16)
        norm_two[chunk, 0] = normal
        norm_two[chunk, 1] = core_swap(normal)
    for chunk in range(CHUNKS):
        halves = []
        for side in range(2):
            spot = chunk, side
            cot[spot] = piece_of(cotangent, chunk, side)
            pre = jnp.dot(norm_two[spot], w_up, preferred_element_type=F32) + c_up
            activated[spot] = gelu_exact(pre).astype(BF16)
            d_act = mm(cot[spot], w_down, NT)
            d_pre[spot] = (d_act * gelu_slope(pre)).astype(BF16)
            c_up_sum = c_up_sum + jnp.sum(d_pre[spot], axis=0, dtype=F32)
            halves.append(mm(d_pre[spot], w_up, NT).astype(BF16))
        chip_sum = add_low(halves[0], core_swap(halves[1]))
        d_norm = chip_sum.astype(F32) + chip_swap(chip_sum).astype(F32)
        d_value, d_gain, d_shift = norm_back(
            d_norm, normed_two[chunk], inv_std_two[chunk], ln2_gain
        )
        gain_two_sum = gain_two_sum + d_gain
        shift_two_sum = shift_two_sum + d_shift
        d_value = cot[chunk, 0].astype(F32) + d_value
        d_attended.append(d_value)
        low = d_value.astype(BF16)
        d_attended_rows[chunk, 0] = low
        d_attended_rows[chunk, 1] = core_swap(low)

    d_heads = {
        spot: mm(d_attended_rows[spot], w_out, NT).astype(BF16) for spot in spots
    }
    d_q, d_kv = attend_back(
        0, core_scalar, slopes, segments, qkv_pieces,
        [d_heads[0, 0], d_heads[0, 1]], heads_out[0], lse[0],
    )
    d_qkv = attend_back(
        1, core_scalar, slopes, segments, qkv_pieces,
        [d_heads[1, 0], d_heads[1, 1]], heads_out[1], lse[1], (d_q, d_kv),
    )

    d_w_down = sum(mm(activated[spot], cot[spot], TN) for spot in spots)
    d_w_up = sum(mm(norm_two[spot], d_pre[spot], TN) for spot in spots)
    d_w_out = sum(
        mm(heads_out[spot[0]][spot[1]], d_attended_rows[spot], TN) for spot in spots
    )
    d_w_down, d_w_up = lax.psum((d_w_down.astype(BF16), d_w_up.astype(BF16)), ("section", "dp"))

    halves = []
    for side in range(2):
        acts = jnp.concatenate(
            [activated[chunk, side].reshape(2, 1, block, -1) for chunk in range(CHUNKS)], axis=1
        ).reshape(2 * CHUNKS * block, -1)
        halves.append(jnp.dot(acts, w_down, preferred_element_type=F32).astype(BF16))
    chip_sum = add_low(halves[0], core_swap(halves[1])).reshape(2, CHUNKS * block, D)
    away = lax.dynamic_index_in_dim(chip_sum, 1 - chip, 0, keepdims=False)
    home = lax.dynamic_index_in_dim(chip_sum, chip, 0, keepdims=False)
    kept = jnp.concatenate(
        [
            lax.dynamic_index_in_dim(value.reshape(2, block, D), chip, 0, keepdims=False)
            for value in attended
        ],
        axis=0,
    )
    layer_out = kept + (home.astype(F32) + chip_swap(away).astype(F32))

    d_merged, d_merged_rows = [], {}
    gain_one_sum = shift_one_sum = skip_sum = 0.0
    for chunk in range(CHUNKS):
        halves = [
            mm(d_qkv[2 * chunk + side], qkv_matrix, NT).astype(BF16) for side in range(2)
        ]
        chip_sum = add_low(halves[0], core_swap(halves[1]))
        d_norm = chip_sum.astype(F32) + chip_swap(chip_sum).astype(F32)
        d_value, d_gain, d_shift = norm_back(
            d_norm, normed_one[chunk], inv_std_one[chunk], ln1_gain
        )
        d_value = d_attended[chunk] + d_value
        gain_one_sum = gain_one_sum + d_gain
        shift_one_sum = shift_one_sum + d_shift
        skip_sum = skip_sum + jnp.sum(d_value, axis=0)
        low = d_value.astype(BF16)
        d_merged_rows[chunk, 0] = low
        d_merged_rows[chunk, 1] = core_swap(low)
    d_w_qkv = sum(mm(norm_one[spot], d_qkv[n], TN) for n, spot in enumerate(spots))

    d_partner = whole_of(
        [mm(d_merged_rows[spot], w_skip[1], NT).astype(BF16) for spot in spots]
    )
    d_encoder_out = partner_swap(d_partner)
    d_w_skip = [
        sum(mm(piece_of(decoder_in, *spot), d_merged_rows[spot], TN) for spot in spots),
        sum(mm(partner_piece(*spot), d_merged_rows[spot], TN) for spot in spots),
    ]
    d_decoder_in = whole_of([mm(d_merged_rows[spot], w_skip[0], NT) for spot in spots])

    steps = group_steps()
    d_w_out, d_w_qkv = d_w_out.astype(BF16), d_w_qkv.astype(BF16)
    late = group_sum(
        jnp.concatenate([d_w_out, d_w_qkv.reshape(3 * local_width, D)], axis=0), steps
    )
    d_w_out, d_w_qkv = late[:local_width], late[local_width:].reshape(w_qkv.shape)
    last = group_sum(jnp.concatenate([part.astype(BF16) for part in d_w_skip], axis=0), steps)
    d_w_skip = last.reshape(w_skip.shape)

    small = jnp.stack([skip_sum, gain_one_sum, shift_one_sum, gain_two_sum, shift_two_sum]) * 0.5
    small = small + core_swap(small)
    small = small + chip_swap(small)
    small = jnp.concatenate([small, c_up_sum[None]], axis=0)
    for axis, bit in steps:
        small = small + swap(small, axis, bit)
    return (
        layer_out,
        d_decoder_in,
        d_encoder_out,
        d_w_skip.astype(F32),
        small[0],
        small[1],
        small[2],
        d_w_qkv.astype(F32),
        d_w_out.astype(F32),
        small[3],
        small[4],
        d_w_up.astype(F32),
        small[5],
        d_w_down.astype(F32),
    )


def solution(mesh):
    return jax.shard_map(
        shards,
        mesh=mesh,
        in_specs=(
            P(("section", "dp"), "tensor"),
            P(("section", "dp"), "tensor"),
            P(("section", "dp"), None),
            P(None, "tensor", None),
            P(),
            P(),
            P(),
            P(None, None, "tensor"),
            P("tensor", None),
            P(),
            P(),
            P(None, "tensor"),
            P("tensor"),
            P("tensor", None),
            P(("section", "dp"), None),
        ),
        out_specs=(
            P(("section", "dp", "tensor"), None),
            P(("section", "dp"), "tensor"),
            P(("section", "dp"), "tensor"),
            P(None, "tensor", None),
            P(),
            P(),
            P(),
            P(None, None, "tensor"),
            P("tensor", None),
            P(),
            P(),
            P(None, "tensor"),
            P("tensor"),
            P("tensor", None),
        ),
        check_vma=False,
    )
```

time: 1440 us -> 605 us (0.42)
  waiting for transfers between devices: 823 us -> 241 us
  matrix products: 275 us -> 109 us
  Pallas kernels: 0 us -> 78.7 us
  local copies, waits for them, and re-layouts: 112 us -> 39.5 us
  other arithmetic: 110 us -> 52 us
  starting transfers between devices: 4.88 us -> 62.5 us
  blocking collectives: 51.1 us -> 0 us
  loops' own time: 34.1 us -> 0 us
    psum x1, waiting for transfers between devices: 400 us -> 0.01 us  [shards(): lax.psum((d_w_down.astype(BF16), d_w_up.astype(BF16)), ('section', 'dp'))]
    reduce_scatter x5 -> x0, waiting for transfers between devices: 296 us -> none  [the longest x1 73.3 us: shards(): lax.psum_scatter(jnp.dot(rows_of(decoder_in, row_start, local_rows * lax....]
    ppermute x2 -> x46, waiting for transfers between devices: 20.8 us -> 241 us  [swap(): return lax.ppermute(value, axis, pairs)]
    dot_general x46 -> x70, matrix products: 275 us -> 109 us  [the longest x48 73.2 us: mm(): return lax.dot_general(left, right, dims, preferred_element_type=F32)]
    all_gather x4 -> x0, waiting for transfers between devices: 105 us -> none  [the longest x1 34.6 us: shards(): lax.all_gather(norm_two.astype(jnp.bfloat16), 'tensor', axis=0, tiled=True)]
    pallas_call x0 -> x4, Pallas kernels: none -> 78.7 us  [the longest x2 50.4 us: attend_back(): pl.pallas_call(functools.partial(bwd_kernel, heads, bk, chunk), out_shape...]
    ppermute x2 -> x46, starting transfers between devices: 4.47 us -> 62.5 us  [swap(): return lax.ppermute(value, axis, pairs)]
    psum x2 -> x0, blocking collectives: 51.1 us -> none  [the longest x1 40 us: shards(): lax.psum((d_w_skip, small_sum, d_w_qkv, d_w_out, d_w_up, d_c_up, d_w_down...]
  transfers between devices with their start and end apart: 12 -> 47, of which waited for: 11 -> 23; matrix products, arithmetic and copies ran while one was open for 4% -> 27% of each run, Pallas kernels for 0% -> 11%
where the time goes in v1:
time: 605 us; the launch traced here: 599 us
  waiting for transfers between devices  241 us (40%)
  matrix products  109 us (18%)
  Pallas kernels  78.7 us (13%)
  starting transfers between devices  62.5 us (10%)
  other arithmetic  52 us (9%)
  local copies, waits for them, and re-layouts  39.5 us (7%)
  between operations  16.1 us (3%)
    ppermute x46, waiting for transfers between devices, swap(): return lax.ppermute(value, axis, pairs)  241 us
    dot_general x48, matrix products, mm(): return lax.dot_general(left, right, dims, preferred_element_type=F32)  73.2 us
    ppermute x46, starting transfers between devices, swap(): return lax.ppermute(value, axis, pairs)  62.5 us
    pallas_call x2, Pallas kernels, attend_back(): pl.pallas_call(functools.partial(bwd_kernel, heads, bk, chunk), out_shape...  50.4 us
    pallas_call x2, Pallas kernels, attend(): pl.pallas_call(functools.partial(fwd_kernel, heads, bk, chunk), out_shape...  28.3 us
    unnamed x205, local copies, waits for them, and re-layouts  14.2 us
  transfers between devices with their start and end apart: 47, of which 23 were waited for; matrix products, arithmetic and copies ran while one was open for 27% of the time, Pallas kernels for 11%

profile of v1, /device:TPU:0, one launch (start us, length us, event | category | flops | bytes accessed | tf_op | source)
XLA Modules:
  0.0 599.2 jit_solution(10936789689874947818)
XLA Ops:
  15.4 10.2 %collective-permute-done.4 = bf16[1024,256]{1,0:T(8,128)(2,1)} collective-permute-done((bf16[1024,256]{1,0:T(8,128)(2,1)}, bf16[1024,256]{1,0:T(8,128)(2,1)}, u32[]{:S(2)}, u32[]{:S(2)}) %collective-permute-start.4) | collective-permute-done | bytes 524320 | tf_op jit(solution)/shard_map/ppermute | solution.py:338
  25.6 10.4 %collective-permute-done = bf16[1024,256]{1,0:T(8,128)(2,1)} collective-permute-done((bf16[1024,256]{1,0:T(8,128)(2,1)}, bf16[1024,256]{1,0:T(8,128)(2,1)}, u32[]{:S(2)}, u32[]{:S(2)}) %collective-permute-start) | collective-permute-done | bytes 524320 | tf_op jit(solution)/shard_map/ppermute | solution.py:338
  44.4 22.7 %collective-permute-done.6 = bf16[512,1024]{1,0:T(8,128)(2,1)S(1)} collective-permute-done((bf16[512,1024]{1,0:T(8,128)(2,1)S(1)}, bf16[512,1024]{1,0:T(8,128)(2,1)S(1)}, u32[]{:S(2)}, u32[]{:S(2)}) %collective-permute-start.6) | collective-permute-done | bytes 1048608 | tf_op jit(solution)/shard_map/ppermute | solution.py:338
  67.1 21.7 %collective-permute-done.2 = bf16[512,1024]{1,0:T(8,128)(2,1)S(1)} collective-permute-done((bf16[512,1024]{1,0:T(8,128)(2,1)S(1)}, bf16[512,1024]{1,0:T(8,128)(2,1)S(1)}, u32[]{:S(2)}, u32[]{:S(2)}) %collective-permute-start.2) | collective-permute-done | bytes 1048608 | tf_op jit(solution)/shard_map/ppermute | solution.py:338
  107.0 13.4 %attend.3 = (bf16[2,512,256]{2,1,0:T(8,128)(2,1)S(1)}, f32[4,4,256]{2,1,0:T(4,128)S(1)}) custom-call(s32[1]{0:T(128)} %bitcast.10.core_ref.refs_0_, f32[4]{0:T(128)S(1)} %multiply_exponential_fusion.slope_ref.refs_1_, s32[1,2048]{1,0:T(1,128)S(1)} %copy-done.10, bf16[2,256,768]{2,1,0:T(8,128)(2,1)S(1)} %bitcast.320, bf16[2,256,768]{2,1,0:T(8,128)(2,1)S(1)} %bitcast.328, ...), custom_call_target="tpu_custom_call" | custom-call | tf_op jit(solution)/shard_map/attend/pallas_call | solution.py:163
  121.0 14.9 %attend.2 = (bf16[2,512,256]{2,1,0:T(8,128)(2,1)S(1)}, f32[4,4,256]{2,1,0:T(4,128)S(1)}) custom-call(s32[1]{0:T(128)} %bitcast.10.core_ref.refs_0_, f32[4]{0:T(128)S(1)} %multiply_exponential_fusion.slope_ref.refs_1_, s32[1,2048]{1,0:T(1,128)S(1)} %copy-done.10, bf16[2,256,768]{2,1,0:T(8,128)(2,1)S(1)} %bitcast.321, bf16[2,256,768]{2,1,0:T(8,128)(2,1)S(1)} %bitcast.329, ...), custom_call_target="tpu_custom_call" | custom-call | tf_op jit(solution)/shard_map/attend/pallas_call | solution.py:163
  152.8 11.8 %collective-permute-done.11 = bf16[512,1024]{1,0:T(8,128)(2,1)} collective-permute-done((bf16[512,1024]{1,0:T(8,128)(2,1)}, bf16[512,1024]{1,0:T(8,128)(2,1)}, u32[]{:S(2)}, u32[]{:S(2)}) %collective-permute-start.11) | collective-permute-done | bytes 1048608 | tf_op jit(solution)/shard_map/ppermute | solution.py:338
  164.6 21.6 %collective-permute-done.9 = bf16[512,1024]{1,0:T(8,128)(2,1)} collective-permute-done((bf16[512,1024]{1,0:T(8,128)(2,1)}, bf16[512,1024]{1,0:T(8,128)(2,1)}, u32[]{:S(2)}, u32[]{:S(2)}) %collective-permute-start.9) | collective-permute-done | bytes 1048608 | tf_op jit(solution)/shard_map/ppermute | solution.py:338
  205.0 6.7 %convert_reduce_fusion.2 = (f32[1024]{0:T(1024)S(1)}, bf16[512,1024]{1,0:T(8,128)(2,1)S(1)}, bf16[512,1024]{1,0:T(8,128)(2,1)S(1)}, bf16[512,1024]{1,0:T(8,128)(...) fusion(f32[512,1024]{1,0:T(8,128)} %fusion.127, ...), kind=kOutput, calls=%fused_computation.42 | convolution fusion | flops 1096808448 | bytes 19935232 | tf_op jit(solution)/shard_map/dot_general | solution.py:519
  245.0 14.2 %collective-permute-done.17 = bf16[512,1024]{1,0:T(8,128)(2,1)} collective-permute-done((bf16[512,1024]{1,0:T(8,128)(2,1)}, bf16[512,1024]{1,0:T(8,128)(2,1)}, u32[]{:S(2)}, u32[]{:S(2)}) %collective-permute-start.17) | collective-permute-done | bytes 1048608 | tf_op jit(solution)/shard_map/ppermute | solution.py:338
  261.9 19.4 %collective-permute-done.19 = bf16[512,1024]{1,0:T(8,128)(2,1)} collective-permute-done((bf16[512,1024]{1,0:T(8,128)(2,1)}, bf16[512,1024]{1,0:T(8,128)(2,1)}, u32[]{:S(2)}, u32[]{:S(2)}) %collective-permute-start.19) | collective-permute-done | bytes 1048608 | tf_op jit(solution)/shard_map/ppermute | solution.py:338
  281.2 4.5 fusion.116
  294.6 25.4 %attend_back.2 = (bf16[2,512,256]{2,1,0:T(8,128)(2,1)S(1)}, f32[2048,512]{1,0:T(8,128)}) custom-call(s32[1]{0:T(128)} %bitcast.10.core_ref.refs_0_, f32[4]{0:T(128)S(1)} %multiply_exponential_fusion.slope_ref.refs_1_, s32[1,2048]{1,0:T(1,128)S(1)} %copy-done.10, bf16[2,256,768]{2,1,0:T(8,128)(2,1)S(1)} %bitcast.322, bf16[2,256,768]{2,1,0:T(8,128)(2,1)S(1)} %bitcast.330, ...), custom_call_target="tpu_custom_call" | custom-call | tf_op jit(solution)/shard_map/attend_back/pallas_call | solution.py:317
  320.6 25.0 %attend_back.3 = bf16[4,512,768]{2,1,0:T(8,128)(2,1)} custom-call(s32[1]{0:T(128)} %bitcast.10.core_ref.refs_0_, f32[4]{0:T(128)S(1)} %multiply_exponential_fusion.slope_ref.refs_1_, s32[1,2048]{1,0:T(1,128)S(1)} %copy-done.10, bf16[2,256,768]{2,1,0:T(8,128)(2,1)S(1)} %bitcast.323, bf16[2,256,768]{2,1,0:T(8,128)(2,1)S(1)} %bitcast.331, ...), custom_call_target="tpu_custom_call" | custom-call | tf_op jit(solution)/shard_map/attend_back/pallas_call | solution.py:317
  379.0 15.0 %collective-permute-done.40 = bf16[512,1024]{1,0:T(8,128)(2,1)S(1)} collective-permute-done((bf16[512,1024]{1,0:T(8,128)(2,1)S(1)}, bf16[512,1024]{1,0:T(8,128)(2,1)S(1)}, u32[]{:S(2)}, u32[]{:S(2)}) %collective-permute-start.40) | collective-permute-done | bytes 1048608 | tf_op jit(solution)/shard_map/ppermute | solution.py:338
  394.4 14.1 %collective-permute-start.41 = (bf16[256,1024]{1,0:T(8,128)(2,1)S(1)}, bf16[256,1024]{1,0:T(8,128)(2,1)S(1)}, u32[]{:S(2)}, u32[]{:S(2)}) collective-permute-start(bf16[256,1024]{1,0:T(8,128)(2,1)S(1)} %dynamic-slice_bitcast_fusion.4), channel_id=1, source_target_pairs={{0,4},{4,0},{8,12},{12,8},{1,5},{5,1},{9,13},{13,9},{2,6},{6,2},{1... | collective-permute-start | bytes 1572872 | tf_op jit(solution)/shard_map/ppermute | solution.py:338
  412.5 7.8 %collective-permute-done.41 = bf16[256,1024]{1,0:T(8,128)(2,1)S(1)} collective-permute-done((bf16[256,1024]{1,0:T(8,128)(2,1)S(1)}, bf16[256,1024]{1,0:T(8,128)(2,1)S(1)}, u32[]{:S(2)}, u32[]{:S(2)}) %collective-permute-start.41) | collective-permute-done | bytes 524320 | tf_op jit(solution)/shard_map/ppermute | solution.py:338
  423.2 4.2 convert_element_type.541
  430.1 5.1 collective-permute-done.42
  436.9 6.9 %collective-permute-done.25 = bf16[512,1024]{1,0:T(8,128)(2,1)} collective-permute-done((bf16[512,1024]{1,0:T(8,128)(2,1)S(1)}, bf16[512,1024]{1,0:T(8,128)(2,1)}, u32[]{:S(2)}, u32[]{:S(2)}) %collective-permute-start.25) | collective-permute-done | bytes 1048608 | tf_op jit(solution)/shard_map/ppermute | solution.py:338
  443.9 4.2 multiply_reduce_fusion.3
  465.4 15.5 %collective-permute-start.44 = (bf16[256,1024]{1,0:T(8,128)(2,1)S(1)}, bf16[256,1024]{1,0:T(8,128)(2,1)S(1)}, u32[]{:S(2)}, u32[]{:S(2)}) collective-permute-start(bf16[256,1024]{1,0:T(8,128)(2,1)S(1)} %pad_maximum_fusion.14), channel_id=1, source_target_pairs={{0,4},{4,0},{8,12},{12,8},{1,5},{5,1},{9,13},{13,9},{2,6},{6,2},{1... | collective-permute-start | bytes 1572872 | tf_op jit(solution)/shard_map/ppermute | solution.py:338
  483.2 9.5 %collective-permute-done.38 = f32[6,1024]{1,0:T(8,128)S(1)} collective-permute-done((f32[6,1024]{1,0:T(8,128)S(1)}, f32[6,1024]{1,0:T(8,128)S(1)}, u32[]{:S(2)}, u32[]{:S(2)}) %collective-permute-start.38) | collective-permute-done | bytes 24608 | tf_op jit(solution)/shard_map/ppermute | solution.py:338
  493.2 4.3 collective-permute-done.39
  505.5 26.7 %collective-permute-done.29 = bf16[256,1024]{1,0:T(8,128)(2,1)S(1)} collective-permute-done((bf16[256,1024]{1,0:T(8,128)(2,1)S(1)}, bf16[256,1024]{1,0:T(8,128)(2,1)S(1)}, u32[]{:S(2)}, u32[]{:S(2)}) %collective-permute-start.29) | collective-permute-done | bytes 524320 | tf_op jit(solution)/shard_map/ppermute | solution.py:338
  535.2 5.0 collective-permute-done.30
  541.1 8.4 %collective-permute-done.31 = bf16[64,1024]{1,0:T(8,128)(2,1)S(1)} collective-permute-done((bf16[64,1024]{1,0:T(8,128)(2,1)S(1)}, bf16[64,1024]{1,0:T(8,128)(2,1)S(1)}, u32[]{:S(2)}, u32[]{:S(2)}) %collective-permute-start.31) | collective-permute-done | bytes 131104 | tf_op jit(solution)/shard_map/ppermute | solution.py:338
  550.1 5.7 collective-permute-done.32
  566.8 5.8 reshape.710
  572.6 4.5 copy.40
  578.2 4.3 collective-permute-done.28
  582.4 5.5 collective-permute-done.34
  (437 shorter events, 208.6 us)
Async XLA Ops:
  7.2 416.0 %all-reduce.3.cloned.1.call-start = ((), (), s32[]{:S(2)}) async-start(), calls=%async_computation | async-start | bytes 8388608 | tf_op jit(solution)/shard_map/psum | solution.py:555
  9.6 16.0 %collective-permute-start.4 = (bf16[1024,256]{1,0:T(8,128)(2,1)}, bf16[1024,256]{1,0:T(8,128)(2,1)}, u32[]{:S(2)}, u32[]{:S(2)}) collective-permute-start(bf16[1024,256]{1,0:T(8,128)(2,1)} %bitcast.15), channel_id=1, source_target_pairs={{0,16},{16,0},{1,17},{17,1},{2,18},{18,2},{3,19},{19,3},{4,20},{20... | collective-permute-start | bytes 1572872 | tf_op jit(solution)/shard_map/ppermute | solution.py:338
  12.6 23.5 %collective-permute-start = (bf16[1024,256]{1,0:T(8,128)(2,1)}, bf16[1024,256]{1,0:T(8,128)(2,1)}, u32[]{:S(2)}, u32[]{:S(2)}) collective-permute-start(bf16[1024,256]{1,0:T(8,128)(2,1)} %bitcast.4), channel_id=1, source_target_pairs={{0,16},{16,0},{1,17},{17,1},{2,18},{18,2},{3,19},{19,3},{4,20},{20... | collective-permute-start | bytes 1572872 | tf_op jit(solution)/shard_map/ppermute | solution.py:338
  41.1 26.1 %collective-permute-start.6 = (bf16[512,1024]{1,0:T(8,128)(2,1)S(1)}, bf16[512,1024]{1,0:T(8,128)(2,1)S(1)}, u32[]{:S(2)}, u32[]{:S(2)}) collective-permute-start(bf16[512,1024]{1,0:T(8,128)(2,1)S(1)} %add_convert_fusion.13), channel_id=1, source_target_pairs={{0,2},{1,3},{2,0},{3,1},{4,6},{5,7},{6,4},{7,5},{8,10},{9,11},{10,... | collective-permute-start | bytes 3145736 | tf_op jit(solution)/shard_map/ppermute | solution.py:338
  43.4 45.4 %collective-permute-start.2 = (bf16[512,1024]{1,0:T(8,128)(2,1)S(1)}, bf16[512,1024]{1,0:T(8,128)(2,1)S(1)}, u32[]{:S(2)}, u32[]{:S(2)}) collective-permute-start(bf16[512,1024]{1,0:T(8,128)(2,1)S(1)} %add_convert_fusion.17), channel_id=1, source_target_pairs={{0,2},{1,3},{2,0},{3,1},{4,6},{5,7},{6,4},{7,5},{8,10},{9,11},{10,... | collective-permute-start | bytes 3145736 | tf_op jit(solution)/shard_map/ppermute | solution.py:338
  120.9 16.0 %collective-permute-start.10 = (bf16[512,1024]{1,0:T(8,128)(2,1)S(1)}, bf16[512,1024]{1,0:T(8,128)(2,1)S(1)}, u32[]{:S(2)}, u32[]{:S(2)}) collective-permute-start(bf16[512,1024]{1,0:T(8,128)(2,1)S(1)} %convolution_convert_fusion.9), channel_id=1, source_target_pairs={{0,1},{1,0},{2,3},{3,2},{4,5},{5,4},{6,7},{7,6},{8,9},{9,8},{10,11... | collective-permute-start | bytes 3145736 | tf_op jit(solution)/shard_map/ppermute | solution.py:338
  138.2 26.3 %collective-permute-start.11 = (bf16[512,1024]{1,0:T(8,128)(2,1)}, bf16[512,1024]{1,0:T(8,128)(2,1)}, u32[]{:S(2)}, u32[]{:S(2)}) collective-permute-start(bf16[512,1024]{1,0:T(8,128)(2,1)} %add_convert_fusion.10), channel_id=1, source_target_pairs={{0,2},{1,3},{2,0},{3,1},{4,6},{5,7},{6,4},{7,5},{8,10},{9,11},{10,... | collective-permute-start | bytes 3145736 | tf_op jit(solution)/shard_map/ppermute | solution.py:338
  141.4 44.7 %collective-permute-start.9 = (bf16[512,1024]{1,0:T(8,128)(2,1)}, bf16[512,1024]{1,0:T(8,128)(2,1)}, u32[]{:S(2)}, u32[]{:S(2)}) collective-permute-start(bf16[512,1024]{1,0:T(8,128)(2,1)} %add_convert_fusion.11), channel_id=1, source_target_pairs={{0,2},{1,3},{2,0},{3,1},{4,6},{5,7},{6,4},{7,5},{8,10},{9,11},{10,... | collective-permute-start | bytes 3145736 | tf_op jit(solution)/shard_map/ppermute | solution.py:338
  191.3 13.7 %collective-permute-start.12 = (bf16[512,1024]{1,0:T(8,128)(2,1)S(1)}, bf16[512,1024]{1,0:T(8,128)(2,1)S(1)}, u32[]{:S(2)}, u32[]{:S(2)}) collective-permute-start(bf16[512,1024]{1,0:T(8,128)(2,1)S(1)} %get-tuple-element.126), channel_id=1, source_target_pairs={{0,1},{1,0},{2,3},{3,2},{4,5},{5,4},{6,7},{7,6},{8,9},{9,8},{10,11... | collective-permute-start | bytes 3145736 | tf_op jit(solution)/shard_map/ppermute | solution.py:338
  216.4 18.3 %collective-permute-start.18 = (bf16[512,1024]{1,0:T(8,128)(2,1)}, bf16[512,1024]{1,0:T(8,128)(2,1)}, u32[]{:S(2)}, u32[]{:S(2)}) collective-permute-start(bf16[512,1024]{1,0:T(8,128)(2,1)} %convolution_convert_fusion.5), channel_id=1, source_target_pairs={{0,1},{1,0},{2,3},{3,2},{4,5},{5,4},{6,7},{7,6},{8,9},{9,8},{10,11... | collective-permute-start | bytes 3145736 | tf_op jit(solution)/shard_map/ppermute | solution.py:338
  216.5 12.8 %collective-permute-start.16 = (bf16[512,1024]{1,0:T(8,128)(2,1)}, bf16[512,1024]{1,0:T(8,128)(2,1)}, u32[]{:S(2)}, u32[]{:S(2)}) collective-permute-start(bf16[512,1024]{1,0:T(8,128)(2,1)} %convolution_convert_fusion.7), channel_id=1, source_target_pairs={{0,1},{1,0},{2,3},{3,2},{4,5},{5,4},{6,7},{7,6},{8,9},{9,8},{10,11... | collective-permute-start | bytes 3145736 | tf_op jit(solution)/shard_map/ppermute | solution.py:338
  222.1 147.2 %collective-permute-start.14 = (bf16[1024,1024]{1,0:T(8,128)(2,1)}, bf16[1024,1024]{1,0:T(8,128)(2,1)}, u32[]{:S(2)}, u32[]{:S(2)}) collective-permute-start(bf16[1024,1024]{1,0:T(8,128)(2,1)} %convolution_convert_fusion), channel_id=1, source_target_pairs={{0,1},{1,0},{2,3},{3,2},{4,5},{5,4},{6,7},{7,6},{8,9},{9,8},{10,11... | collective-permute-start | bytes 6291464 | tf_op jit(solution)/shard_map/ppermute | solution.py:338
  232.9 26.3 %collective-permute-start.17 = (bf16[512,1024]{1,0:T(8,128)(2,1)}, bf16[512,1024]{1,0:T(8,128)(2,1)}, u32[]{:S(2)}, u32[]{:S(2)}) collective-permute-start(bf16[512,1024]{1,0:T(8,128)(2,1)} %add_convert_fusion.7), channel_id=1, source_target_pairs={{0,2},{1,3},{2,0},{3,1},{4,6},{5,7},{6,4},{7,5},{8,10},{9,11},{10,... | collective-permute-start | bytes 3145736 | tf_op jit(solution)/shard_map/ppermute | solution.py:338
  238.4 42.9 %collective-permute-start.19 = (bf16[512,1024]{1,0:T(8,128)(2,1)}, bf16[512,1024]{1,0:T(8,128)(2,1)}, u32[]{:S(2)}, u32[]{:S(2)}) collective-permute-start(bf16[512,1024]{1,0:T(8,128)(2,1)} %add_convert_fusion.6), channel_id=1, source_target_pairs={{0,2},{1,3},{2,0},{3,1},{4,6},{5,7},{6,4},{7,5},{8,10},{9,11},{10,... | collective-permute-start | bytes 3145736 | tf_op jit(solution)/shard_map/ppermute | solution.py:338
  289.7 30.4 %collective-permute-start.20 = (bf16[512,1024]{1,0:T(8,128)(2,1)S(1)}, bf16[512,1024]{1,0:T(8,128)(2,1)S(1)}, u32[]{:S(2)}, u32[]{:S(2)}) collective-permute-start(bf16[512,1024]{1,0:T(8,128)(2,1)S(1)} %get-tuple-element.76), channel_id=1, source_target_pairs={{0,1},{1,0},{2,3},{3,2},{4,5},{5,4},{6,7},{7,6},{8,9},{9,8},{10,11... | collective-permute-start | bytes 3145736 | tf_op jit(solution)/shard_map/ppermute | solution.py:338
  353.2 22.2 %collective-permute-start.22 = (bf16[512,1024]{1,0:T(8,128)(2,1)}, bf16[512,1024]{1,0:T(8,128)(2,1)}, u32[]{:S(2)}, u32[]{:S(2)}) collective-permute-start(bf16[512,1024]{1,0:T(8,128)(2,1)} %convolution_convert_fusion.3), channel_id=1, source_target_pairs={{0,1},{1,0},{2,3},{3,2},{4,5},{5,4},{6,7},{7,6},{8,9},{9,8},{10,11... | collective-permute-start | bytes 3145736 | tf_op jit(solution)/shard_map/ppermute | solution.py:338
  353.3 55.3 %collective-permute-start.24 = (bf16[512,1024]{1,0:T(8,128)(2,1)}, bf16[512,1024]{1,0:T(8,128)(2,1)}, u32[]{:S(2)}, u32[]{:S(2)}) collective-permute-start(bf16[512,1024]{1,0:T(8,128)(2,1)} %convolution_convert_fusion.1), channel_id=1, source_target_pairs={{0,1},{1,0},{2,3},{3,2},{4,5},{5,4},{6,7},{7,6},{8,9},{9,8},{10,11... | collective-permute-start | bytes 3145736 | tf_op jit(solution)/shard_map/ppermute | solution.py:338
  367.4 26.5 %collective-permute-start.40 = (bf16[512,1024]{1,0:T(8,128)(2,1)S(1)}, bf16[512,1024]{1,0:T(8,128)(2,1)S(1)}, u32[]{:S(2)}, u32[]{:S(2)}) collective-permute-start(bf16[512,1024]{1,0:T(8,128)(2,1)S(1)} %dynamic-slice_bitcast_fusion), channel_id=1, source_target_pairs={{0,16},{16,0},{1,17},{17,1},{2,18},{18,2},{3,19},{19,3},{4,20},{20... | collective-permute-start | bytes 3145736 | tf_op jit(solution)/shard_map/ppermute | solution.py:338
  373.6 47.7 %collective-permute-start.15 = (bf16[512,1024]{1,0:T(8,128)(2,1)S(1)}, bf16[512,1024]{1,0:T(8,128)(2,1)S(1)}, u32[]{:S(2)}, u32[]{:S(2)}) collective-permute-start(bf16[512,1024]{1,0:T(8,128)(2,1)S(1)} %dynamic-slice_bitcast_fusion.1), channel_id=1, source_target_pairs={{0,2},{1,3},{2,0},{3,1},{4,6},{5,7},{6,4},{7,5},{8,10},{9,11},{10,... | collective-permute-start | bytes 3145736 | tf_op jit(solution)/shard_map/ppermute | solution.py:338
  377.7 59.3 %collective-permute-start.23 = (bf16[512,1024]{1,0:T(8,128)(2,1)S(1)}, bf16[512,1024]{1,0:T(8,128)(2,1)}, u32[]{:S(2)}, u32[]{:S(2)}) collective-permute-start(bf16[512,1024]{1,0:T(8,128)(2,1)S(1)} %add_convert_fusion.5), channel_id=1, source_target_pairs={{0,2},{1,3},{2,0},{3,1},{4,6},{5,7},{6,4},{7,5},{8,10},{9,11},{10,... | collective-permute-start | bytes 3145736 | tf_op jit(solution)/shard_map/ppermute | solution.py:338
  394.4 25.8 %collective-permute-start.41 = (bf16[256,1024]{1,0:T(8,128)(2,1)S(1)}, bf16[256,1024]{1,0:T(8,128)(2,1)S(1)}, u32[]{:S(2)}, u32[]{:S(2)}) collective-permute-start(bf16[256,1024]{1,0:T(8,128)(2,1)S(1)} %dynamic-slice_bitcast_fusion.4), channel_id=1, source_target_pairs={{0,4},{4,0},{8,12},{12,8},{1,5},{5,1},{9,13},{13,9},{2,6},{6,2},{1... | collective-permute-start | bytes 1572872 | tf_op jit(solution)/shard_map/ppermute | solution.py:338
  410.9 33.0 %collective-permute-start.25 = (bf16[512,1024]{1,0:T(8,128)(2,1)S(1)}, bf16[512,1024]{1,0:T(8,128)(2,1)}, u32[]{:S(2)}, u32[]{:S(2)}) collective-permute-start(bf16[512,1024]{1,0:T(8,128)(2,1)S(1)} %add_convert_fusion.4), channel_id=1, source_target_pairs={{0,2},{1,3},{2,0},{3,1},{4,6},{5,7},{6,4},{7,5},{8,10},{9,11},{10,... | collective-permute-start | bytes 3145736 | tf_op jit(solution)/shard_map/ppermute | solution.py:338
  421.3 14.0 %collective-permute-start.42 = (bf16[128,1024]{1,0:T(8,128)(2,1)S(1)}, bf16[128,1024]{1,0:T(8,128)(2,1)}, u32[]{:S(2)}, u32[]{:S(2)}) collective-permute-start(bf16[128,1024]{1,0:T(8,128)(2,1)S(1)} %dynamic-slice_bitcast_fusion.6), channel_id=1, source_target_pairs={{0,8},{4,12},{8,0},{12,4},{1,9},{5,13},{9,1},{13,5},{2,10},{6,14},... | collective-permute-start | bytes 786440 | tf_op jit(solution)/shard_map/ppermute | solution.py:338
  436.9 24.4 %collective-permute-start.43 = (bf16[128,1024]{1,0:T(8,128)(2,1)}, bf16[128,1024]{1,0:T(8,128)(2,1)}, u32[]{:S(2)}, u32[]{:S(2)}) collective-permute-start(bf16[128,1024]{1,0:T(8,128)(2,1)} %fusion.50), channel_id=1, source_target_pairs={{0,8},{4,12},{8,0},{12,4},{1,9},{5,13},{9,1},{13,5},{2,10},{6,14},... | collective-permute-start | bytes 786440 | tf_op jit(solution)/shard_map/ppermute | solution.py:338
  459.0 39.9 %collective-permute-start.27 = (bf16[512,1024]{1,0:T(8,128)(2,1)S(1)}, bf16[512,1024]{1,0:T(8,128)(2,1)S(1)}, u32[]{:S(2)}, u32[]{:S(2)}) collective-permute-start(bf16[512,1024]{1,0:T(8,128)(2,1)S(1)} %copy-done.32), channel_id=1, source_target_pairs={{0,1},{1,0},{2,3},{3,2},{4,5},{5,4},{6,7},{7,6},{8,9},{9,8},{10,11... | collective-permute-start | bytes 3145736 | tf_op jit(solution)/shard_map/ppermute | solution.py:338
  459.4 40.1 %collective-permute-start.26 = (bf16[512,1024]{1,0:T(8,128)(2,1)S(1)}, bf16[512,1024]{1,0:T(8,128)(2,1)S(1)}, u32[]{:S(2)}, u32[]{:S(2)}) collective-permute-start(bf16[512,1024]{1,0:T(8,128)(2,1)S(1)} %get-tuple-element.69), channel_id=1, source_target_pairs={{0,1},{1,0},{2,3},{3,2},{4,5},{5,4},{6,7},{7,6},{8,9},{9,8},{10,11... | collective-permute-start | bytes 3145736 | tf_op jit(solution)/shard_map/ppermute | solution.py:338
  463.5 17.4 %collective-permute-start.37 = (f32[6,1024]{1,0:T(8,128)S(1)}, f32[6,1024]{1,0:T(8,128)S(1)}, u32[]{:S(2)}, u32[]{:S(2)}) collective-permute-start(f32[6,1024]{1,0:T(8,128)S(1)} %pad_maximum_fusion.16), channel_id=1, source_target_pairs={{0,16},{16,0},{1,17},{17,1},{2,18},{18,2},{3,19},{19,3},{4,20},{20... | collective-permute-start | bytes 73736 | tf_op jit(solution)/shard_map/ppermute | solution.py:338
  465.4 32.8 %collective-permute-start.44 = (bf16[256,1024]{1,0:T(8,128)(2,1)S(1)}, bf16[256,1024]{1,0:T(8,128)(2,1)S(1)}, u32[]{:S(2)}, u32[]{:S(2)}) collective-permute-start(bf16[256,1024]{1,0:T(8,128)(2,1)S(1)} %pad_maximum_fusion.14), channel_id=1, source_target_pairs={{0,4},{4,0},{8,12},{12,8},{1,5},{5,1},{9,13},{13,9},{2,6},{6,2},{1... | collective-permute-start | bytes 1572872 | tf_op jit(solution)/shard_map/ppermute | solution.py:338
  498.5 65.6 %collective-permute-start.45 = (bf16[512,1024]{1,0:T(8,128)(2,1)S(1)}, bf16[512,1024]{1,0:T(8,128)(2,1)S(1)}, u32[]{:S(2)}, u32[]{:S(2)}) collective-permute-start(bf16[512,1024]{1,0:T(8,128)(2,1)S(1)} %pad_maximum_fusion.10), channel_id=1, source_target_pairs={{0,16},{16,0},{1,17},{17,1},{2,18},{18,2},{3,19},{19,3},{4,20},{20... | collective-permute-start | bytes 3145736 | tf_op jit(solution)/shard_map/ppermute | solution.py:338
  502.9 29.2 %collective-permute-start.29 = (bf16[256,1024]{1,0:T(8,128)(2,1)S(1)}, bf16[256,1024]{1,0:T(8,128)(2,1)S(1)}, u32[]{:S(2)}, u32[]{:S(2)}) collective-permute-start(bf16[256,1024]{1,0:T(8,128)(2,1)S(1)} %dynamic-slice_bitcast_fusion.5), channel_id=1, source_target_pairs={{0,16},{16,0},{1,17},{17,1},{2,18},{18,2},{3,19},{19,3},{4,20},{20... | collective-permute-start | bytes 1572872 | tf_op jit(solution)/shard_map/ppermute | solution.py:338
  557.8 24.7 %collective-permute-start.28 = (bf16[2048,256]{1,0:T(8,128)(2,1)}, bf16[2048,256]{1,0:T(8,128)(2,1)}, u32[]{:S(2)}, u32[]{:S(2)}) collective-permute-start(bf16[2048,256]{1,0:T(8,128)(2,1)} %bitcast.66), channel_id=1, source_target_pairs={{0,16},{16,0},{1,17},{17,1},{2,18},{18,2},{3,19},{19,3},{4,20},{20... | collective-permute-start | bytes 3145736 | tf_op jit(solution)/shard_map/ppermute | solution.py:338
  563.3 24.7 %collective-permute-start.34 = (bf16[256,1024]{1,0:T(8,128)(2,1)}, bf16[256,1024]{1,0:T(8,128)(2,1)S(1)}, u32[]{:S(2)}, u32[]{:S(2)}) collective-permute-start(bf16[256,1024]{1,0:T(8,128)(2,1)} %pad_maximum_fusion.13), channel_id=1, source_target_pairs={{0,16},{16,0},{1,17},{17,1},{2,18},{18,2},{3,19},{19,3},{4,20},{20... | collective-permute-start | bytes 1572872 | tf_op jit(solution)/shard_map/ppermute | solution.py:338
  (116 other events, 1456.4 us)
Sparse Core Ops, SparseCore 0:
  242.1 161.8 all-reduce.2
